TPU v7x, 128 devices: a whole 4x4x4 slice. The times are simulated.
128 devices in a mesh: tm: 32 (over z, x, y_hi), rows: 4 (over y_lo, core).
Axes of the slice: x: 4, y: 4 (y_hi: 2, y_lo: 2; y = y_hi * 2 + y_lo), z: 4, core: 2. Of those that a mesh axis runs over, the one named last changes fastest.
Arguments:
- video: bfloat16 [256, 32, 128, 128], P('tm', 'rows'), may hold values from -36 to 50
- conv_weight: bfloat16 [3, 3, 3, 128, 256], replicated, may hold values from -0.109375 to 0.109375
- norm_gain: float32 [256], replicated, may hold values from 0.5 to 1.5
- norm_bias: float32 [256], replicated, may hold values from -3 to 3
Outputs:
- patch_tokens: bfloat16 [16, 64, 256, 1024], P('rows', 'tm')
All inputs are finite; a program needn't handle non-finite values.
Results may differ from a plain program's by a relative error of at most 0.0049.
Values may be sent and summed in bfloat16 or wider, within the bound.
A program may use at most 128 MiB of HBM per device.

v0:
```python
import jax
import jax.numpy as jnp
from jax import lax
from jax.sharding import PartitionSpec as P

GROUPS = 32


inv_root = 0.7071067811865476


def from_partner(block, axis, distance):
    count = lax.axis_size(axis)
    route = []
    for low in range(count):
        high = low | 1 << distance
        if high != low and high < count:
            route += [(low, high), (high, low)]
    return lax.ppermute(block, axis, route)


def shifted(block, axis, distance):
    devices = range(lax.axis_size(axis))
    route = [(i - distance, i) for i in devices if i - distance in devices]
    return lax.ppermute(block, axis, route)


def padded_2(cells, sides, width):
    for axis, dim in sides:
        count = lax.axis_size(axis)
        ends = count - 1
        head = lax.slice_in_dim(cells, 0, width, axis=dim)
        tail = lax.slice_in_dim(cells, cells.shape[dim] - width, cells.shape[dim], axis=dim)
        cells = jnp.concatenate(
            [
                lax.ppermute(tail, axis, [(i, (i + 1) % count) for i in range(ends)]),
                cells,
                lax.ppermute(head, axis, [((i + 1) % count, i) for i in range(ends)]),
            ],
            axis=dim,
        )
    return cells


def per_device(video, conv_weight, norm_gain, norm_bias):
    frames, height, width, channels = video.shape
    tm_count = lax.axis_size("tm")
    current = video.astype(jnp.float32)
    position = lax.axis_index("tm")
    for bit_number in range(3):
        partner = from_partner(current, "tm", bit_number)
        is_upper = position >> bit_number & 1 == 1
        current = jnp.where(
            is_upper, (partner - current) * inv_root, (current + partner) * inv_root
        )
    wavelet = current.astype(jnp.bfloat16)
    last_frames = wavelet[frames - 2 :]
    earlier = shifted(last_frames, "tm", 1)
    extended = jnp.concatenate([earlier, wavelet], axis=0)
    with_rows = padded_2(extended, (("rows", 1),), 1)
    padded = jnp.pad(with_rows, ((0, 0), (0, 0), (1, 1), (0, 0)))
    convolved = lax.conv_general_dilated(
        padded[None],
        conv_weight,
        (1, 1, 1),
        "VALID",
        dimension_numbers=("NDHWC", "DHWIO", "NDHWC"),
        preferred_element_type=jnp.float32,
    )[0]
    out_frames, out_height, out_width, out_channels = convolved.shape
    group_count = GROUPS
    groups = convolved.reshape(
        out_frames, out_height, out_width, group_count, out_channels // group_count
    )
    entries = float(
        out_frames
        * out_height
        * out_width
        * (out_channels // group_count)
        * tm_count
        * lax.axis_size("rows")
    )
    local_sums = jnp.sum(groups, axis=(0, 1, 2, 4))
    group_total = lax.psum(local_sums, ("tm", "rows"))
    group_mean = group_total / entries
    centered = groups - group_mean[:, None]
    squares = lax.psum(jnp.sum(centered * centered, axis=(0, 1, 2, 4)), ("tm", "rows"))
    variance = squares / entries
    normed = (centered / jnp.sqrt(variance + 1e-05)[:, None]).reshape(
        out_frames, out_height, out_width, out_channels
    )
    activated = jax.nn.silu(normed * norm_gain + norm_bias).astype(jnp.bfloat16)
    arranged = activated.reshape(
        out_frames, out_height // 2, 2, out_width // 2, 2, out_channels
    ).transpose(1, 3, 0, 2, 4, 5)
    arranged = arranged.reshape(out_height // 2, out_width // 2, out_frames, 4 * out_channels)
    return lax.all_to_all(arranged, "tm", split_axis=1, concat_axis=2, tiled=True)


def solution(mesh):
    placed = (P("tm", "rows", None, None), P(), P(), P())
    return jax.shard_map(
        per_device,
        mesh=mesh,
        in_specs=placed,
        out_specs=P("rows", "tm", None, None),
        check_vma=False,
    )
```

profile of v0, /device:TPU:0, one launch (start us, length us, event | category | flops | bytes accessed | tf_op | source)
XLA Modules:
  0.0 597.1 jit_solution(17662172223809165032)
XLA Ops:
  0.0 4.3 convert_element_type.12
  4.3 3.3 collective-permute-start
  7.5 90.9 %collective-permute-done = f32[8,8,128,128]{3,2,1,0:T(8,128)} collective-permute-done((f32[8,8,128,128]{3,2,1,0:T(8,128)}, f32[8,8,128,128]{3,2,1,0:T(8,128)}, u32[]{:S(2)}, u32[]{:S(2)}) %collective-permute-start) | collective-permute-done | bytes 4194336 | tf_op jit(solution)/shard_map/ppermute | solution.py:19
  98.4 5.9 multiply_select_fusion.1
  104.3 1.5 collective-permute-start.1
  105.9 90.2 %collective-permute-done.1 = f32[8,8,128,128]{3,2,1,0:T(8,128)} collective-permute-done((f32[8,8,128,128]{3,2,1,0:T(8,128)}, f32[8,8,128,128]{3,2,1,0:T(8,128)}, u32[]{:S(2)}, u32[]{:S(2)}) %collective-permute-start.1) | collective-permute-done | bytes 4194336 | tf_op jit(solution)/shard_map/ppermute | solution.py:19
  196.1 6.9 %multiply_select_fusion = f32[8,8,128,128]{3,2,1,0:T(8,128)} fusion(f32[8,8,128,128]{3,2,1,0:T(8,128)} %multiply_select_fusion.1, f32[8,8,128,128]{3,2,1,0:T(8,128)} %collective-permute-done.1, pred[]{:T(512)S(6)} %eq.10), kind=kLoop, calls=%fused_computation.15 | loop fusion | flops 5242880 | bytes 12582913 | tf_op jit(solution)/shard_map/jit(_where)/select_n | solution.py:53
  203.0 3.0 collective-permute-start.2
  206.1 89.3 %collective-permute-done.2 = f32[8,8,128,128]{3,2,1,0:T(8,128)} collective-permute-done((f32[8,8,128,128]{3,2,1,0:T(8,128)}, f32[8,8,128,128]{3,2,1,0:T(8,128)}, u32[]{:S(2)}, u32[]{:S(2)}) %collective-permute-start.2) | collective-permute-done | bytes 4194336 | tf_op jit(solution)/shard_map/ppermute | solution.py:19
  295.4 4.5 select_convert_fusion
  299.9 5.1 collective-permute-start.3
  305.1 8.4 %collective-permute-done.3 = bf16[2,8,128,128]{3,2,1,0:T(8,128)(2,1)S(1)} collective-permute-done((bf16[2,8,128,128]{3,2,1,0:T(8,128)(2,1)S(1)}, bf16[2,8,128,128]{3,2,1,0:T(8,128)(2,1)S(1)}, u32[]{:S(2)}, u32[]{:S(2)}) %collective-permute-start.3) | collective-permute-done | bytes 524320 | tf_op jit(solution)/shard_map/ppermute | solution.py:25
  313.5 1.3 collective-permute-start.4
  314.9 1.3 collective-permute-start.5
  316.2 3.1 collective-permute-done.5
  319.3 2.1 fusion.13
  321.4 2.0 pad.5
  323.4 6.9 %reshape.19 = bf16[10,10,1,8,17,128]{5,4,3,1,0,2:T(8,128)(2,1)} reshape(bf16[10,10,1,136,128]{4,3,1,0,2:T(8,128)(2,1)} %pad.5) | data formatting | bytes 6963200 | tf_op jit(solution)/shard_map/conv_general_dilated | solution.py:62
  330.4 3.0 copy.29
  333.5 19.0 %select_reduce_fusion.1 = (f32[256]{0:T(256)S(1)}, f32[8,8,8,17,256]{4,2,3,1,0:T(8,128)}) fusion(pred[8,17]{0,1:T(8,128)(4,1)S(1)} %copy-done.3, bf16[3,3,3,128,256]{4,3,2,1,0:T(8,128)(2,1)S(1)} %copy-done, bf16[10,10,1,7,2,128]{5,3,4,1,0,2:T(8,128)(2,1)S(1)} %slice.15, bf16[10,10,1,8,17,128]{5,3,4,1,0,2:T(8,128)(2,1)S(1)} %copy.29), kind=kOutput, calls=%fused_computation.3 | convolution fusion | flops 15419842560 | bytes 14523528 | tf_op jit(solution)/shard_map/conv_general_dilated | solution.py:62
  352.7 0.1 reduce_sum.25
  352.8 75.9 %psum.14 = f32[32]{0:T(128)S(1)} all-reduce(f32[32]{0:T(128)S(1)} %reduce_sum.25), channel_id=1, replica_groups=mesh['tm'=32,'rows'=4] {'tm','rows'}, use_global_device_ids=true, to_apply=%region_2.3 | all-reduce | flops 32 | bytes 256 | tf_op jit(solution)/shard_map/psum | solution.py:84
  428.9 6.3 %copy.30 = f32[8,8,8,17,256]{4,1,3,2,0:T(8,128)S(1)} copy(f32[8,8,8,17,256]{4,2,3,1,0:T(8,128)} %get-tuple-element.8) | data formatting | bytes 17825792 | tf_op jit(solution)/shard_map/conv_general_dilated | solution.py:62
  435.2 1.5 select_reduce_fusion
  436.8 4.1 slice.16
  441.0 11.5 %copy.31 = f32[8,8,1,128,256]{4,0,3,1,2:T(8,128)} copy(f32[8,8,1,128,256]{4,1,3,0,2:T(8,128)} %slice.16) | data formatting | bytes 16777216 | tf_op jit(solution)/shard_map/conv_general_dilated | solution.py:62
  452.5 62.4 %psum.15 = f32[32]{0:T(128)S(1)} all-reduce(f32[32]{0:T(128)S(1)} %reduce_sum.37), channel_id=1, replica_groups=mesh['tm'=32,'rows'=4] {'tm','rows'}, use_global_device_ids=true, to_apply=%region_5.6 | all-reduce | flops 32 | bytes 256 | tf_op jit(solution)/shard_map/psum | solution.py:87
  515.2 6.9 %fusion.5 = bf16[4,64,8,2,2,256]{5,1,4,3,0,2:T(8,128)(2,1)S(1)} fusion(f32[256]{0:T(256)S(1)} %copy-done.4, f32[256]{0:T(256)S(1)} %copy-done.5, f32[256]{0:T(256)S(1)} %div.28, f32[256]{0:T(256)S(1)} %sub.32, f32[8,4,2,64,2,256]{5,0,4,3,2,1:T(8,128)} %bitcast.27), kind=kLoop, calls=%fused_computation.17 | loop fusion | flops 18874368 | bytes 12587008 | tf_op jit(solution)/shard_map/transpose | solution.py:95
  522.0 6.4 %copy.37 = bf16[4,64,8,2,2,256]{5,4,3,2,0,1:T(2,128)(2,1)} copy(bf16[4,64,8,2,2,256]{5,1,4,3,0,2:T(8,128)(2,1)S(1)} %fusion.5) | data formatting | bytes 8388608 | tf_op jit(solution)/shard_map/reshape | solution.py:96
  528.4 7.7 %reshape.33 = bf16[4,64,8,1024]{3,2,0,1:T(8,128)(2,1)} reshape(bf16[4,64,8,2,2,256]{5,4,3,2,0,1:T(2,128)(2,1)} %copy.37) | data formatting | bytes 8388608 | tf_op jit(solution)/shard_map/reshape | solution.py:96
  536.1 58.5 %all_to_all.18 = bf16[4,64,8,1024]{3,2,0,1:T(8,128)(2,1)S(1)} all-to-all(bf16[4,64,8,1024]{3,2,0,1:T(8,128)(2,1)} %reshape.33), channel_id=1, replica_groups=mesh['tm'=32,'rows'=4] {'tm'}, dimensions={1} | all-to-all | bytes 8388608 | tf_op jit(solution)/shard_map/all_to_all | solution.py:97
  594.6 2.5 copy.52
  (25 shorter events, 0.8 us)
Async XLA Ops:
  0.0 333.5 %copy-start = (bf16[3,3,3,128,256]{4,3,2,1,0:T(8,128)(2,1)S(1)}, bf16[3,3,3,128,256]{4,3,2,1,0:T(8,128)(2,1)}, u32[]{:S(2)}) copy-start(bf16[3,3,3,128,256]{4,3,2,1,0:T(8,128)(2,1)} %param.5) | copy-start | bytes 5308420
  4.3 94.2 %collective-permute-start = (f32[8,8,128,128]{3,2,1,0:T(8,128)}, f32[8,8,128,128]{3,2,1,0:T(8,128)}, u32[]{:S(2)}, u32[]{:S(2)}) collective-permute-start(f32[8,8,128,128]{3,2,1,0:T(8,128)} %convert_element_type.12), channel_id=1, source_target_pairs={{0,4},{4,0},{8,12},{12,8},{16,20},{20,16},{24,28},{28,24},{32,36},... | collective-permute-start | bytes 12582920 | tf_op jit(solution)/shard_map/ppermute | solution.py:19
  104.3 91.8 %collective-permute-start.1 = (f32[8,8,128,128]{3,2,1,0:T(8,128)}, f32[8,8,128,128]{3,2,1,0:T(8,128)}, u32[]{:S(2)}, u32[]{:S(2)}) collective-permute-start(f32[8,8,128,128]{3,2,1,0:T(8,128)} %multiply_select_fusion.1), channel_id=1, source_target_pairs={{0,8},{8,0},{4,12},{12,4},{16,24},{24,16},{20,28},{28,20},{32,40},... | collective-permute-start | bytes 12582920 | tf_op jit(solution)/shard_map/ppermute | solution.py:19
  203.0 92.4 %collective-permute-start.2 = (f32[8,8,128,128]{3,2,1,0:T(8,128)}, f32[8,8,128,128]{3,2,1,0:T(8,128)}, u32[]{:S(2)}, u32[]{:S(2)}) collective-permute-start(f32[8,8,128,128]{3,2,1,0:T(8,128)} %multiply_select_fusion), channel_id=1, source_target_pairs={{0,16},{16,0},{4,20},{20,4},{8,24},{24,8},{12,28},{28,12},{32,48},... | collective-permute-start | bytes 12582920 | tf_op jit(solution)/shard_map/ppermute | solution.py:19
  299.9 13.5 %collective-permute-start.3 = (bf16[2,8,128,128]{3,2,1,0:T(8,128)(2,1)S(1)}, bf16[2,8,128,128]{3,2,1,0:T(8,128)(2,1)S(1)}, u32[]{:S(2)}, u32[]{:S(2)}) collective-permute-start(bf16[2,8,128,128]{3,2,1,0:T(8,128)(2,1)S(1)} %slice.14), channel_id=1, source_target_pairs={{0,4},{4,8},{8,12},{12,16},{16,20},{20,24},{24,28},{28,32},{32,36}... | collective-permute-start | bytes 1572872 | tf_op jit(solution)/shard_map/ppermute | solution.py:25
  313.5 2.6 collective-permute-start.4
  314.9 4.4 collective-permute-start.5
  330.4 3.2 copy-start.3
  428.8 6.4 %copy-start.2 = (f32[8,8,8,17,256]{4,2,3,1,0:T(8,128)S(1)}, f32[8,8,8,17,256]{4,2,3,1,0:T(8,128)}, u32[]{:S(2)}) copy-start(f32[8,8,8,17,256]{4,2,3,1,0:T(8,128)} %get-tuple-element.8) | copy-start | bytes 26738692
  441.0 74.1 %copy-start.4 = (f32[256]{0:T(256)S(1)}, f32[256]{0:T(256)}, u32[]{:S(2)}) copy-start(f32[256]{0:T(256)} %param.7) | copy-start | bytes 3076
  441.0 74.1 %copy-start.5 = (f32[256]{0:T(256)S(1)}, f32[256]{0:T(256)}, u32[]{:S(2)}) copy-start(f32[256]{0:T(256)} %param.6) | copy-start | bytes 3076
  594.6 2.5 copy-start.1
where the time goes:
time: 598 us; the launch traced here: 597 us
  waiting for transfers between devices  282 us (47%)
  blocking collectives  197 us (33%)
  local copies, waits for them, and re-layouts  51 us (9%)
  other arithmetic  32.4 us (5%)
  matrix products  19 us (3%)
  starting transfers between devices  15.6 us (3%)
    ppermute x3, waiting for transfers between devices, from_partner(): return lax.ppermute(block, axis, route)  270 us
    psum x1, blocking collectives, per_device(): group_total = lax.psum(local_sums, ('tm', 'rows'))  75.9 us
    psum x1, blocking collectives, per_device(): lax.psum(jnp.sum(centered * centered, axis=(0, 1, 2, 4)), ('tm', 'rows'))  62.4 us
    all_to_all x1, blocking collectives, per_device(): lax.all_to_all(arranged, 'tm', split_axis=1, concat_axis=2, tiled=True)  58.5 us
    conv_general_dilated x6, local copies, waits for them, and re-layouts, per_device(): lax.conv_general_dilated(padded[None], conv_weight, (1, 1, 1), 'VALID', d...  31.9 us
    conv_general_dilated x1, matrix products, per_device(): lax.conv_general_dilated(padded[None], conv_weight, (1, 1, 1), 'VALID', d...  19 us
    reshape x2, local copies, waits for them, and re-layouts, per_device(): arranged.reshape(out_height // 2, out_width // 2, out_frames, 4 * out_cha...  14.1 us
    select_n x2, other arithmetic, per_device(): jnp.where(is_upper, (partner - current) * inv_root, (current + partner) *...  12.8 us
  transfers between devices with their start and end apart: 6, of which 5 were waited for; matrix products, arithmetic and copies ran while one was open for 0% of the time, Pallas kernels for 0%

commit v1 on v0

v1 whole, which is shorter than its diff:
```python
import jax
import jax.numpy as jnp
from jax import lax
from jax.experimental import pallas as pl
from jax.experimental.pallas import tpu as pltpu
from jax.sharding import PartitionSpec as P

MESH = pl.DeviceIdType.MESH
F32 = jnp.float32
BF16 = jnp.bfloat16

NZ, NX, NY, NR = 4, 4, 2, 4
C = 128
CO = 256
HALF_ROOT = 0.35355339059327373
T_ROWS = 272
RANGES = {0: (16, 48), 1: (64, 64), 3: (208, 64), 2: (128, 80)}
PIECES = {0: ((16, 48),), 1: ((64, 64),), 3: ((208, 48), (256, 16)), 2: ((128, 64), (192, 16))}


def exchange_conv(
    video, weight, gain, bias,
    conv_out, norm_out,
    src, zbuf, xbuf, ybuf, edge, halo, wave, taps, acc, w_vmem, st,
    z_s, z_r, x_s, x_r, y_s, y_r, l_s, h_s, h_r, st_s, st_r, w_s, o_s,
):
    me = lax.axis_index("tm")
    r = lax.axis_index("rows")
    z, x, y = me // 8, (me // 2) % 4, me % 2

    def at(z, x, y):
        return {"tm": z * 8 + x * 2 + y}

    weights = pltpu.make_async_copy(weight, w_vmem, w_s)
    weights.start()

    barrier = pltpu.get_barrier_semaphore()
    for d in (1, 2, 3):
        for peer in (at((z + d) % 4, x, y), at(z, (x + d) % 4, y), {"rows": (r + d) % 4}):
            pl.semaphore_signal(barrier, inc=1, device_id=peer, device_id_type=MESH)
    pl.semaphore_signal(barrier, inc=1, device_id=at(z, x, 1 - y), device_id_type=MESH)

    src[0] = jnp.zeros((64, C), BF16)
    src[129] = jnp.zeros((64, C), BF16)

    def turn(pair, carry):
        rows = pl.ds(pl.multiple_of(pair * 16, 16), 16)
        for w0 in range(0, 128, 32):
            two = [jnp.swapaxes(video[:, 2 * pair + k, pl.ds(w0, 32), :], 0, 1) for k in range(2)]
            src[pl.ds(1 + w0, 32), rows, :] = jnp.concatenate(two, axis=1)
        return carry

    lax.fori_loop(0, 4, turn, 0)

    @pl.when(r == 0)
    def _():
        halo[:, 0] = jnp.zeros((4, 6, 64, C), BF16)

    @pl.when(r == 3)
    def _():
        halo[:, 1] = jnp.zeros((4, 6, 64, C), BF16)

    pl.semaphore_wait(barrier, 10)

    def zcopy(s):
        zp = (z - s) % 4
        return pltpu.make_async_remote_copy(
            src_ref=src.at[pl.ds(32 * zp, 34)], dst_ref=zbuf.at[s - 1],
            send_sem=z_s.at[s - 1], recv_sem=z_r.at[s - 1],
            device_id=at(zp, x, y), device_id_type=MESH)

    def zcols(s, first, n):
        return src.at[pl.ds(32 * z + first, n)] if s == 0 else zbuf.at[s - 1, pl.ds(first, n)]

    def xcopy(s, d):
        xp = (x + d) % 4
        return pltpu.make_async_remote_copy(
            src_ref=zcols(s, 8 * xp, 10), dst_ref=xbuf.at[s, x],
            send_sem=x_s.at[s, d], recv_sem=x_r.at[s, d],
            device_id=at(z, xp, y), device_id_type=MESH)

    def xlocal(s):
        return pltpu.make_async_copy(zcols(s, 8 * x, 10), xbuf.at[s, x], l_s.at[s])

    def ycopy(s, d):
        xs = (x - d) % 4
        if isinstance(d, int) and d == 0:
            part = zcols(s, 8 * x + 4 * (1 - y), 6)
        else:
            part = xbuf.at[s, xs, pl.ds(4 * (1 - y), 6)]
        return pltpu.make_async_remote_copy(
            src_ref=part, dst_ref=ybuf.at[s, xs],
            send_sem=y_s.at[s, d], recv_sem=y_r.at[s, d],
            device_id=at(z, x, 1 - y), device_id_type=MESH)

    def begin(s):
        for d in (1, 3, 2):
            xcopy(s, d).start()
        xlocal(s).start()
        ycopy(s, 0).start()

    def forward(s, d):
        xcopy(s, d).wait_recv()
        ycopy(s, d).start()

    def up(s):
        return pltpu.make_async_remote_copy(
            src_ref=edge.at[s, 0], dst_ref=halo.at[s, 1],
            send_sem=h_s.at[s, 0], recv_sem=h_r.at[s, 1],
            device_id={"rows": r - 1}, device_id_type=MESH)

    def down(s):
        return pltpu.make_async_remote_copy(
            src_ref=edge.at[s, 1], dst_ref=halo.at[s, 0],
            send_sem=h_s.at[s, 1], recv_sem=h_r.at[s, 0],
            device_id={"rows": r + 1}, device_id_type=MESH)

    sign = jnp.where(y == 0, HALF_ROOT, -HALF_ROOT).astype(F32)

    def packet(s, w, h0, n):
        rows = pl.ds(h0 * 8, n * 8)
        even, odd = [], []
        for xs in range(4):
            a = xbuf[s, xs, 4 * y + w, rows, :].astype(F32)
            b = ybuf[s, xs, w, rows, :].astype(F32)
            even.append((a + b) * HALF_ROOT)
            odd.append((a - b) * sign)
        out = [None] * 8
        for side, v in ((0, even), (1, odd)):
            p, q, u, t = v[0] + v[1], v[0] - v[1], v[2] + v[3], v[2] - v[3]
            out[0 + side], out[4 + side] = p + u, p - u
            out[2 + side], out[6 + side] = q + t, q - t
        return out

    def waves(s):
        def column(w, carry):
            for h0 in (0, 4):
                blocks = packet(s, w, h0, 4)
                for k in range(4):
                    h = h0 + k
                    line = jnp.concatenate([b[8 * k : 8 * k + 8] for b in blocks], axis=0)
                    wave[w, h + 1, 8 + 64 * s : 72 + 64 * s, :] = line
                    if s == 0:
                        wave[w, h + 1, 264:280, :] = line[:16]
                    if h in (0, 7):
                        edge[s, 0 if h == 0 else 1, w] = line.astype(BF16)
            return carry

        lax.fori_loop(0, 6, column, 0)

        @pl.when(r > 0)
        def _():
            up(s).start()

        @pl.when(r < 3)
        def _():
            down(s).start()

    clip_start = 256 - 64 * z

    def build_taps(s, h_from, h_to):
        r0, n = RANGES[s]
        row = r0 + lax.broadcasted_iota(jnp.int32, (n, C), 0) - clip_start
        outside = [(row >= 0) & (row < 2), row == 0, None]

        def line(i, carry):
            h = h_from + i // 6
            w = i % 6
            for k in range(3):
                v = wave[w, h, 8 + r0 + k - 2 : 8 + r0 + k - 2 + n, :]
                if k < 2:
                    v = jnp.where(outside[k], 0.0, v)
                taps[k, w, h, r0 : r0 + n, :] = v.astype(BF16)
            return carry

        lax.fori_loop(0, 6 * (h_to - h_from), line, 0)

    def take_halo(s):
        @pl.when(r > 0)
        def _():
            down(s).wait_recv()

        @pl.when(r < 3)
        def _():
            up(s).wait_recv()

        def column(w, carry):
            for side, h in ((0, 0), (1, 9)):
                line = halo[s, side, w].astype(F32)
                wave[w, h, 8 + 64 * s : 72 + 64 * s, :] = line
                if s == 0:
                    wave[w, h, 264:280, :] = line[:16]
            return carry

        lax.fori_loop(0, 6, column, 0)

    count = [0]
    st[0] = jnp.zeros((8, CO), F32)

    def add_stats(out, m):
        mean = jnp.sum(out, axis=0, keepdims=True) * (1.0 / m)
        d = out - mean
        return mean, jnp.sum(d * d, axis=0, keepdims=True)

    def merge(a, b):
        (na, ma, qa), (nb, mb, qb) = a, b
        n = na + nb
        delta = mb - ma
        return n, ma + delta * (nb / n), qa + qb + delta * delta * (na * nb / n)

    def conv_pairs(s, hooks):
        r0, n = RANGES[s]

        def chunk(m, carry):
            h = 1 + 2 * m
            parts = []
            for k in range(3):
                for i in range(3):
                    for j in range(3):
                        v = taps[k, j : j + 4, pl.ds(h + i, 2), r0 : r0 + n, :]
                        parts.append(v.reshape(8 * n, C))
            out = jnp.dot(jnp.concatenate(parts, axis=1), w_vmem[...], preferred_element_type=F32)
            for w in range(4):
                for a in range(2):
                    piece = out[(2 * w + a) * n : (2 * w + a + 1) * n]
                    lane = ((1 - a) * 2 + w % 2) * CO
                    acc[m + a, w // 2, r0 : r0 + n, lane : lane + CO] = piece
            mean, sq = add_stats(out, 8 * n)
            st[1, pl.ds(m, 1), :] = mean
            st[2, pl.ds(m, 1), :] = sq
            if hooks is not None:
                hooks(m)
            return carry

        lax.fori_loop(0, 3, chunk, 0)

    def conv_edges(s):
        r0, n = RANGES[s]
        parts = []
        for k in range(3):
            for i in range(3):
                for j in range(3):
                    top = taps[k, j : j + 4, i, r0 : r0 + n, :].reshape(4 * n, C)
                    low = taps[k, j : j + 4, 7 + i, r0 : r0 + n, :].reshape(4 * n, C)
                    parts.append(jnp.concatenate([top, low], axis=0))
        out = jnp.dot(jnp.concatenate(parts, axis=1), w_vmem[...], preferred_element_type=F32)
        for w in range(4):
            for a, p in ((0, 0), (1, 3)):
                piece = out[(4 * a + w) * n : (4 * a + w + 1) * n]
                lane = (a * 2 + w % 2) * CO
                acc[p, w // 2, r0 : r0 + n, lane : lane + CO] = piece
        mean, sq = add_stats(out, 8 * n)
        st[1, 3:4, :] = mean
        st[2, 3:4, :] = sq

    def out_copies(s):
        copies = []
        for i, (first, n) in enumerate(PIECES[s]):
            t = (64 * z + first) % 256
            copies.append(
                pltpu.make_async_copy(
                    acc.at[:, :, pl.ds(first, n), :],
                    conv_out.at[:, :, pl.ds(pl.multiple_of(t, 16), n), :],
                    o_s.at[s, i]))
        return copies

    def finish(s):
        n = 8 * RANGES[s][1]
        total = None
        for m in range(4):
            term = (n, st[1, m : m + 1, :], st[2, m : m + 1, :])
            total = term if total is None else merge(total, term)
        if count[0]:
            total = merge((count[0], st[0, 0:1, :], st[0, 1:2, :]), total)
        st[0, 0:1, :] = total[1]
        st[0, 1:2, :] = total[2]
        count[0] = total[0]
        for copy in out_copies(s):
            copy.start()

    def arrive(s):
        xlocal(s).wait()
        for d in range(4):
            ycopy(s, d).wait_recv()

    def hook(s):
        def run(m):
            forward(s, 1 + 2 * m - 3 * (m // 2))
        return run

    def stage(s, hooks):
        arrive(s)
        waves(s)
        build_taps(s, 1, 9)
        conv_pairs(s, hooks)
        take_halo(s)
        build_taps(s, 0, 1)
        build_taps(s, 9, 10)
        conv_edges(s)
        finish(s)

    zcopy(1).start()
    zcopy(3).start()
    begin(0)
    for d in (1, 3, 2):
        forward(0, d)
    zcopy(1).wait_recv()
    begin(1)
    zcopy(3).wait_recv()
    zcopy(1).wait_send()
    zcopy(3).wait_send()
    zcopy(2).start()
    begin(3)
    weights.wait()
    stage(0, hook(1))
    stage(1, hook(3))
    zcopy(2).wait_recv()
    begin(2)
    stage(3, hook(2))
    stage(2, None)

    mean, sq = st[0, 0:1, :], st[0, 1:2, :]
    held = float(count[0])
    axes = (
        (NR, r, lambda d: {"rows": (r + d) % 4}, lambda d: (r + d) % 4),
        (NY, y, lambda d: at(z, x, (y + d) % 2), lambda d: (y + d) % 2),
        (NX, x, lambda d: at(z, (x + d) % 4, y), lambda d: (x + d) % 4),
        (NZ, z, lambda d: at((z + d) % 4, x, y), lambda d: (z + d) % 4),
    )
    for level, (size, mine, peer, _) in enumerate(axes):
        base = 3 + 4 * level
        st[base + mine, 0:1, :] = mean
        st[base + mine, 1:2, :] = sq

        def share(d):
            return pltpu.make_async_remote_copy(
                src_ref=st.at[base + mine], dst_ref=st.at[base + mine],
                send_sem=st_s.at[level, d], recv_sem=st_r.at[level, d],
                device_id=peer(d), device_id_type=MESH)

        for d in range(1, size):
            share(d).start()
        for d in range(1, size):
            share(d).wait_recv()
        means = [st[base + i, 0:1, :] for i in range(size)]
        mean = sum(means) * (1.0 / size)
        sq = sum(st[base + i, 1:2, :] for i in range(size))
        sq = sq + held * sum((m - mean) * (m - mean) for m in means)
        held = held * size
        for d in range(1, size):
            share(d).wait_send()

    lane = lax.broadcasted_iota(jnp.int32, (1, CO), 1)

    def over_group(v):
        for bit in (1, 2, 4):
            v = v + jnp.where(lane & bit == 0, pltpu.roll(v, CO - bit, 1), pltpu.roll(v, bit, 1))
        return v

    group_mean = over_group(mean) * (1.0 / 8)
    d = mean - group_mean
    variance = over_group(sq + held * d * d) * (1.0 / (8 * held))
    scale = gain[...] / jnp.sqrt(variance + 1e-05)
    for row, v in enumerate((group_mean, scale, bias[...])):
        norm_out[row : row + 1, :] = jnp.concatenate([v] * 4, axis=1)

    for s in range(4):
        for copy in out_copies(s):
            copy.wait()
        for d in range(4):
            ycopy(s, d).wait_send()
        for d in (1, 2, 3):
            xcopy(s, d).wait_send()

        @pl.when(r > 0)
        def _():
            up(s).wait_send()

        @pl.when(r < 3)
        def _():
            down(s).wait_send()
    zcopy(2).wait_send()


def norm_silu(conv, norm, out):
    half = (conv[...] - norm[0:1, :]) * (0.5 * norm[1:2, :]) + 0.5 * norm[2:3, :]
    out[...] = (half + half * jnp.tanh(half)).astype(BF16)


def per_device(video, conv_weight, norm_gain, norm_bias):
    vmem = pl.BlockSpec(memory_space=pltpu.VMEM)
    anywhere = pl.BlockSpec(memory_space=pl.ANY)
    dma = pltpu.SemaphoreType.DMA
    conv, norm = pl.pallas_call(
        exchange_conv,
        out_shape=(
            jax.ShapeDtypeStruct((4, 2, 256, 1024), F32),
            jax.ShapeDtypeStruct((8, 1024), F32),
        ),
        in_specs=[vmem, anywhere, vmem, vmem],
        out_specs=(anywhere, vmem),
        scratch_shapes=[
            pltpu.VMEM((130, 64, C), BF16),
            pltpu.VMEM((3, 34, 64, C), BF16),
            pltpu.VMEM((4, 4, 10, 64, C), BF16),
            pltpu.VMEM((4, 4, 6, 64, C), BF16),
            pltpu.VMEM((4, 2, 6, 64, C), BF16),
            pltpu.VMEM((4, 2, 6, 64, C), BF16),
            pltpu.VMEM((6, 10, 8 + T_ROWS, C), F32),
            pltpu.VMEM((3, 6, 10, T_ROWS, C), BF16),
            pltpu.VMEM((4, 2, T_ROWS, 1024), F32),
            pltpu.VMEM((27 * C, CO), BF16),
            pltpu.VMEM((19, 8, CO), F32),
            dma((3,)), dma((3,)),
            dma((4, 4)), dma((4, 4)),
            dma((4, 4)), dma((4, 4)),
            dma((4,)),
            dma((4, 2)), dma((4, 2)),
            dma((4, 4)), dma((4, 4)),
            dma, dma((4, 2)),
        ],
        compiler_params=pltpu.CompilerParams(
            collective_id=0, has_side_effects=True, vmem_limit_bytes=60 << 20
        ),
        cost_estimate=pl.CostEstimate(
            flops=2 * 8192 * 3456 * 256, bytes_accessed=16 << 20, transcendentals=0
        ),
    )(video, conv_weight.reshape(27 * C, CO), norm_gain.reshape(1, CO), norm_bias.reshape(1, CO))
    return pl.pallas_call(
        norm_silu,
        out_shape=jax.ShapeDtypeStruct((4, 2, 256, 1024), BF16),
        grid=(4, 2),
        in_specs=[
            pl.BlockSpec((1, 1, 256, 1024), lambda p, q: (p, q, 0, 0)),
            pl.BlockSpec((8, 1024), lambda p, q: (0, 0)),
        ],
        out_specs=pl.BlockSpec((1, 1, 256, 1024), lambda p, q: (p, q, 0, 0)),
        compiler_params=pltpu.CompilerParams(vmem_limit_bytes=16 << 20),
        cost_estimate=pl.CostEstimate(
            flops=2097152 * 6, bytes_accessed=12 << 20, transcendentals=2097152
        ),
    )(conv, norm)


def solution(mesh):
    placed = (P("tm", "rows", None, None), P(), P(), P())
    return jax.shard_map(
        per_device,
        mesh=mesh,
        in_specs=placed,
        out_specs=P("rows", "tm", None, None),
        check_vma=False,
    )
```

time: 598 us -> 92.4 us (0.15)
  waiting for transfers between devices: 282 us -> 0 us
  blocking collectives: 197 us -> 0 us
  Pallas kernels: 0 us -> 87 us
  local copies, waits for them, and re-layouts: 51 us -> 4.13 us
  other arithmetic: 32.4 us -> 0 us
  matrix products: 19 us -> 0 us
  starting transfers between devices: 15.6 us -> 0 us
    ppermute x6 -> x0, waiting for transfers between devices: 282 us -> none  [the longest x3 270 us: from_partner(): return lax.ppermute(block, axis, route)]
    psum x2 -> x0, blocking collectives: 138 us -> none  [the longest x1 75.9 us: per_device(): group_total = lax.psum(local_sums, ('tm', 'rows'))]
    pallas_call x0 -> x2, Pallas kernels: none -> 87 us  [the longest x1 82.6 us: per_device(): pl.pallas_call(exchange_conv, out_shape=(jax.ShapeDtypeStruct((4, 2, 256,...]
    all_to_all x1 -> x0, blocking collectives: 58.5 us -> none  [per_device(): lax.all_to_all(arranged, 'tm', split_axis=1, concat_axis=2, tiled=True)]
    conv_general_dilated x6 -> x0, local copies, waits for them, and re-layouts: 31.9 us -> none  [per_device(): lax.conv_general_dilated(padded[None], conv_weight, (1, 1, 1), 'VALID', d...]
    conv_general_dilated x1 -> x0, matrix products: 19 us -> none  [per_device(): lax.conv_general_dilated(padded[None], conv_weight, (1, 1, 1), 'VALID', d...]
    ppermute x6 -> x0, starting transfers between devices: 15.6 us -> none  [the longest x3 7.87 us: from_partner(): return lax.ppermute(block, axis, route)]
    reshape x2 -> x0, local copies, waits for them, and re-layouts: 14.1 us -> none  [per_device(): arranged.reshape(out_height // 2, out_width // 2, out_frames, 4 * out_cha...]
  transfers between devices with their start and end apart: 6 -> 0, of which waited for: 5 -> 0; matrix products, arithmetic and copies ran while one was open for 0% -> 0% of each run, Pallas kernels for 0% -> 0%
where the time goes in v1:
time: 92.4 us; the launch traced here: 91.1 us
  Pallas kernels  87 us (94%)
  local copies, waits for them, and re-layouts  4.13 us (4%)
    pallas_call x1, Pallas kernels, per_device(): pl.pallas_call(exchange_conv, out_shape=(jax.ShapeDtypeStruct((4, 2, 256,...  82.6 us
    pallas_call x1, Pallas kernels, per_device(): pl.pallas_call(norm_silu, out_shape=jax.ShapeDtypeStruct((4, 2, 256, 1024...  4.36 us
    unnamed x4, local copies, waits for them, and re-layouts  4.13 us

profile of v1, /device:TPU:0, one launch (start us, length us, event | category | flops | bytes accessed | tf_op | source)
XLA Modules:
  0.0 91.1 jit_solution(1116674624097948630)
XLA Ops:
  0.0 82.6 %shard_map.46 = (f32[4,2,256,1024]{3,2,1,0:T(8,128)}, f32[8,1024]{1,0:T(8,128)}) custom-call(bf16[8,8,128,128]{3,2,1,0:T(8,128)(2,1)} %video.1, bf16[3456,256]{1,0:T(8,128)(2,1)} %bitcast.3, f32[1,256]{1,0:T(1,128)} %bitcast.4, f32[1,256]{1,0:T(1,128)} %bitcast.5), custom_call_target="tpu_custom_call" | custom-call | flops 14495514624 | bytes 16777216 | tf_op jit(solution)/shard_map/pallas_call | solution.py:394
  82.6 0.0 copy-start
  82.6 3.4 %copy-done = f32[4,2,256,1024]{3,2,1,0:T(8,128)S(1)} copy-done((f32[4,2,256,1024]{3,2,1,0:T(8,128)S(1)}, f32[4,2,256,1024]{3,2,1,0:T(8,128)}, u32[]{:S(2)}) %copy-start) | copy-done | bytes 8388632
  86.0 0.0 copy-start.1
  86.0 0.8 copy-done.1
  86.8 4.4 %shard_map.47 = bf16[4,2,256,1024]{3,2,1,0:T(8,128)(2,1)} custom-call(f32[4,2,256,1024]{3,2,1,0:T(8,128)S(1)} %copy-done, f32[8,1024]{1,0:T(8,128)S(1)} %copy-done.1), custom_call_target="tpu_custom_call" | custom-call | flops 12582912 | bytes 12582912 | tf_op jit(solution)/shard_map/pallas_call | solution.py:429
Async XLA Ops:
  82.6 3.4 %copy-start = (f32[4,2,256,1024]{3,2,1,0:T(8,128)S(1)}, f32[4,2,256,1024]{3,2,1,0:T(8,128)}, u32[]{:S(2)}) copy-start(f32[4,2,256,1024]{3,2,1,0:T(8,128)} %get-tuple-element.7.conv) | copy-start | bytes 25165828
  86.0 0.8 copy-start.1

commit v2 on v1

v2 whole, which is shorter than its diff:
```python
import jax
import jax.numpy as jnp
from jax import lax
from jax.experimental import pallas as pl
from jax.experimental.pallas import tpu as pltpu
from jax.sharding import PartitionSpec as P

MESH = pl.DeviceIdType.MESH
F32 = jnp.float32
BF16 = jnp.bfloat16

C = 128
CO = 256
HALF_ROOT = 0.35355339059327373
T_ROWS = 272
RANGES = {0: (16, 48), 1: (64, 64), 3: (208, 64), 2: (128, 80)}
ORDER = [(0, 1), (0, 3), (0, 2)] + [(s, d) for s in (1, 3, 2) for d in (0, 1, 3, 2)]
PIECES = {0: ((16, 48),), 1: ((64, 64),), 3: ((208, 48), (256, 16)), 2: ((128, 64), (192, 16))}


def exchange_conv(
    video_in, weight, gain, bias,
    conv_out, scale_out, shift_out,
    video, src, xbuf, ybuf, edge, halo, wave, taps, acc, w_vmem, st, sums, ref_mean,
    x_s, x_r, y_s, y_r, l_s, h_s, h_r, st_s, st_r, v_s, w_s, o_s,
):
    me = lax.axis_index("tm")
    r = lax.axis_index("rows")
    z, x, y = me // 8, (me // 2) % 4, me % 2

    def at(z, x, y):
        return {"tm": z * 8 + x * 2 + y}

    frames = pltpu.make_async_copy(video_in, video, v_s)
    frames.start()
    barrier = pltpu.get_barrier_semaphore()
    line_of = lambda i: {"tm": z * 8 + x * 2 + ((y + i // 4) & 1), "rows": (r + i) & 3}
    plane_of = lambda i: at((z + i // 4) & 3, (x + i) & 3, y)
    for peer in [line_of(i) for i in range(1, 8)] + [plane_of(i) for i in range(1, 16)]:
        pl.semaphore_signal(barrier, inc=1, device_id=peer, device_id_type=MESH)

    weights = pltpu.make_async_copy(weight, w_vmem, w_s)
    weights.start()

    src[0] = jnp.zeros((64, C), BF16)
    src[129] = jnp.zeros((64, C), BF16)

    def turn(pair, carry):
        rows = pl.ds(pl.multiple_of(pair * 16, 16), 16)
        for w0 in range(0, 128, 32):
            two = [jnp.swapaxes(video[:, 2 * pair + k, pl.ds(w0, 32), :], 0, 1) for k in range(2)]
            src[pl.ds(1 + w0, 32), rows, :] = jnp.concatenate(two, axis=1)
        return carry

    frames.wait()
    lax.fori_loop(0, 4, turn, 0)

    @pl.when(r == 0)
    def _():
        halo[:, 0] = jnp.zeros((4, 6, 64, C), BF16)

    @pl.when(r == 3)
    def _():
        halo[:, 1] = jnp.zeros((4, 6, 64, C), BF16)

    pl.semaphore_wait(barrier, 22)

    def plane(s, d):
        zp, xp = (z - s) & 3, (x + d) & 3
        return pltpu.make_async_remote_copy(
            src_ref=src.at[pl.ds(32 * zp + 8 * xp, 10)], dst_ref=xbuf.at[s, x],
            send_sem=x_s.at[s, d], recv_sem=x_r.at[s, d],
            device_id=at(zp, xp, y), device_id_type=MESH)

    own = pltpu.make_async_copy(src.at[pl.ds(32 * z + 8 * x, 10)], xbuf.at[0, x], l_s)

    def across(s, d, first=False, c0=0, n=6, row=None):
        xs = (x - d) & 3
        if first:
            part = src.at[pl.ds(32 * z + 8 * x + 4 * (1 - y), 6)]
        else:
            part = xbuf.at[s, xs, pl.ds(4 * (1 - y) + c0, n)]
        row = s if row is None else row
        return pltpu.make_async_remote_copy(
            src_ref=part, dst_ref=ybuf.at[s, xs, pl.ds(c0, n)],
            send_sem=y_s.at[row, d], recv_sem=y_r.at[row, d],
            device_id=at(z, x, 1 - y), device_id_type=MESH)

    def last_a(d):
        return across(2, d, False, 0, 4, 2)

    def last_b(d):
        return across(2, d, False, 4, 2, 4)

    def forward(s, d):
        plane(s, d).wait_recv()
        (last_a(d) if s == 2 else across(s, d)).start()

    def up(s, c0, n, row):
        return pltpu.make_async_remote_copy(
            src_ref=edge.at[s, 0, pl.ds(c0, n)], dst_ref=halo.at[s, 1, pl.ds(c0, n)],
            send_sem=h_s.at[row, 0], recv_sem=h_r.at[row, 1],
            device_id={"rows": r - 1}, device_id_type=MESH)

    def down(s, c0, n, row):
        return pltpu.make_async_remote_copy(
            src_ref=edge.at[s, 1, pl.ds(c0, n)], dst_ref=halo.at[s, 0, pl.ds(c0, n)],
            send_sem=h_s.at[row, 1], recv_sem=h_r.at[row, 0],
            device_id={"rows": r + 1}, device_id_type=MESH)

    sign = jnp.where(y == 0, HALF_ROOT, -HALF_ROOT).astype(F32)

    def packet(s, w, h0, n):
        rows = pl.ds(h0 * 8, n * 8)
        even, odd = [], []
        for xs in range(4):
            a = xbuf[s, xs, 4 * y + w, rows, :].astype(F32)
            b = ybuf[s, xs, w, rows, :].astype(F32)
            even.append((a + b) * HALF_ROOT)
            odd.append((a - b) * sign)
        out = [None] * 8
        for side, v in ((0, even), (1, odd)):
            p, q, u, t = v[0] + v[1], v[0] - v[1], v[2] + v[3], v[2] - v[3]
            out[0 + side], out[4 + side] = p + u, p - u
            out[2 + side], out[6 + side] = q + t, q - t
        return out

    def waves(s, c0, n, row):
        def column(w, carry):
            for h0 in (0, 4):
                blocks = packet(s, w, h0, 4)
                for k in range(4):
                    h = h0 + k
                    line = jnp.concatenate([b[8 * k : 8 * k + 8] for b in blocks], axis=0)
                    wave[w, h + 1, 8 + 64 * s : 72 + 64 * s, :] = line
                    if s == 0:
                        wave[w, h + 1, 264:280, :] = line[:16]
                    if h in (0, 7):
                        edge[s, 0 if h == 0 else 1, w] = line.astype(BF16)
            return carry

        lax.fori_loop(c0, c0 + n, column, 0)

        @pl.when(r > 0)
        def _():
            up(s, c0, n, row).start()

        @pl.when(r < 3)
        def _():
            down(s, c0, n, row).start()

    clip_start = 256 - 64 * z

    def build_taps(s, c0, cn, h_from, h_to):
        r0, n = RANGES[s]
        row = r0 + lax.broadcasted_iota(jnp.int32, (n, C), 0) - clip_start
        outside = [(row >= 0) & (row < 2), row == 0, None]

        def line(h, carry):
            for w in range(c0, c0 + cn):
                for k in range(3):
                    v = wave[w, h, 8 + r0 + k - 2 : 8 + r0 + k - 2 + n, :]
                    if k < 2:
                        v = jnp.where(outside[k], 0.0, v)
                    taps[k, w, h, r0 : r0 + n, :] = v.astype(BF16)
            return carry

        lax.fori_loop(h_from, h_to, line, 0)

    def take_halo(s, c0, n, row):
        @pl.when(r > 0)
        def _():
            down(s, c0, n, row).wait_recv()

        @pl.when(r < 3)
        def _():
            up(s, c0, n, row).wait_recv()

        def column(w, carry):
            for side, h in ((0, 0), (1, 9)):
                line = halo[s, side, w].astype(F32)
                wave[w, h, 8 + 64 * s : 72 + 64 * s, :] = line
                if s == 0:
                    wave[w, h, 264:280, :] = line[:16]
            return carry

        lax.fori_loop(c0, c0 + n, column, 0)

    noted = []

    def merge(a, b):
        (na, ma, qa), (nb, mb, qb) = a, b
        n = na + nb
        delta = mb - ma
        return n, ma + delta * (nb / n), qa + qb + delta * delta * (na * nb / n)

    def conv(s, w0, nw, rows, slot, first=None):
        r0, n = RANGES[s]
        parts = []
        for k in range(3):
            for i in range(3):
                for j in range(3):
                    group = [
                        taps[k, w0 + j : w0 + j + nw, pl.ds(h + i, c), r0 : r0 + n, :].reshape(nw * c * n, C)
                        for h, c in rows
                    ]
                    parts.append(group[0] if len(group) == 1 else jnp.concatenate(group, axis=0))
        out = jnp.dot(jnp.concatenate(parts, axis=1), w_vmem[...], preferred_element_type=F32)
        m = out.shape[0]
        mean = jnp.sum(out, axis=0, keepdims=True) * (1.0 / m)
        d = out - mean
        st[1, pl.ds(slot, 1), :] = mean
        st[2, pl.ds(slot, 1), :] = jnp.sum(d * d, axis=0, keepdims=True)
        if first is not None:
            @pl.when(first)
            def _():
                ref_mean[...] = mean

        kept = (out - ref_mean[...]).astype(BF16)
        pieces, base = [], 0
        for h, c in rows:
            pieces.append(kept[base : base + nw * c * n].reshape(nw, c, n, CO))
            base += nw * c * n
        return pieces

    def conv_pairs(s, hooks):
        r0, n = RANGES[s]

        def chunk(m, carry):
            [piece] = conv(s, 0, 4, [(1 + 2 * m, 2)], m, m == 0 if s == 0 else None)
            for w in range(4):
                for a in range(2):
                    lane = ((1 - a) * 2 + w % 2) * CO
                    acc[m + a, w // 2, r0 : r0 + n, lane : lane + CO] = piece[w, a]
            if hooks is not None:
                hooks(m)
            return carry

        lax.fori_loop(0, 3, chunk, 0)
        noted.extend((8 * n, m) for m in range(3))

    def conv_all(s, w0, nw, rows, slot):
        r0, n = RANGES[s]
        pieces = conv(s, w0, nw, rows, slot)
        for (h, c), piece in zip(rows, pieces):
            for w in range(nw):
                for a in range(c):
                    lane = ((h + a) % 2 * 2 + (w0 + w) % 2) * CO
                    acc[(h + a) // 2, (w0 + w) // 2, r0 : r0 + n, lane : lane + CO] = piece[w, a]
        noted.append((nw * sum(c for _, c in rows) * n, slot))

    EDGES = [(0, 1), (7, 1)]

    def out_copies(s):
        copies = []
        for i, (first, n) in enumerate(PIECES[s]):
            t = (64 * z + first) % 256
            copies.append(
                pltpu.make_async_copy(
                    acc.at[:, :, pl.ds(first, n), :],
                    conv_out.at[:, :, pl.ds(pl.multiple_of(t, 16), n), :],
                    o_s.at[s, i]))
        return copies

    def finish(s):
        total = None if s == 0 else (done[0], st[0, 0:1, :], st[0, 1:2, :])
        for n, slot in noted:
            term = (n, st[1, slot : slot + 1, :], st[2, slot : slot + 1, :])
            total = term if total is None else merge(total, term)
        noted.clear()
        st[0, 0:1, :] = total[1]
        st[0, 1:2, :] = total[2]
        done[0] = total[0]
        for copy in out_copies(s):
            copy.start()

    done = [0]

    def arrive(s):
        if s == 0:
            own.wait()
        for d in range(4):
            across(s, d).wait_recv()

    def hook(*three):
        def run(m):
            for i, (s, d) in enumerate(three):
                @pl.when(m == i)
                def _(s=s, d=d):
                    forward(s, d)

        return run

    def stage(s, hooks):
        arrive(s)
        waves(s, 0, 6, s)
        build_taps(s, 0, 6, 1, 9)
        conv_pairs(s, hooks)
        take_halo(s, 0, 6, s)
        build_taps(s, 0, 6, 0, 1)
        build_taps(s, 0, 6, 9, 10)
        conv_all(s, 0, 4, EDGES, 3)
        finish(s)

    def last_whole(s):
        for d in range(4):
            last_a(d).wait_recv()
            last_b(d).wait_recv()
        waves(s, 0, 6, s)
        build_taps(s, 0, 6, 1, 9)
        conv_pairs(s, None)
        take_halo(s, 0, 6, s)
        build_taps(s, 0, 6, 0, 1)
        build_taps(s, 0, 6, 9, 10)
        conv_all(s, 0, 4, EDGES, 3)
        finish(s)

    for s, d in ORDER:
        plane(s, d).start()
    own.start()
    across(0, 0, True).start()
    for d in (1, 3, 2):
        forward(0, d)
    forward(1, 0)
    weights.wait()
    stage(0, hook((1, 1), (1, 3), (1, 2)))
    for d in (0, 1, 3):
        forward(3, d)
    stage(1, hook((3, 2), (2, 0), (2, 1)))
    for d in (3, 2):
        forward(2, d)
    for d in range(4):
        last_b(d).start()
    stage(3, None)
    last_whole(2)

    mean, sq = st[0, 0:1, :], st[0, 1:2, :]
    held = float(done[0])
    axes = (
        (8, 4 * y + r, line_of, lambda i: 4 * ((y + i // 4) & 1) + ((r + i) & 3)),
        (16, 4 * z + x, plane_of, lambda i: 4 * ((z + i // 4) & 3) + ((x + i) & 3)),
    )
    base, shares = 0, []
    for level, (size, mine, peer, slot) in enumerate(axes):
        sums[base + mine, :, :CO] = mean
        sums[base + mine, :, CO:] = sq
        here = [
            pltpu.make_async_remote_copy(
                src_ref=sums.at[base + mine], dst_ref=sums.at[base + mine],
                send_sem=st_s.at[level, i], recv_sem=st_r.at[level, i],
                device_id=peer(i), device_id_type=MESH)
            for i in range(1, size)
        ]
        for share in here:
            share.start()
        for share in here:
            share.wait_recv()
        shares += here
        means = [sums[base + i, :, :CO] for i in range(size)]
        mean = sum(means) * (1.0 / size)
        sq = sum(sums[base + i, :, CO:] for i in range(size))
        sq = sq + held * sum((m - mean) * (m - mean) for m in means)
        held = held * size
        base += size

    lane = lax.broadcasted_iota(jnp.int32, (1, CO), 1)

    def over_group(v):
        for bit in (1, 2, 4):
            v = v + jnp.where(lane & bit == 0, pltpu.roll(v, CO - bit, 1), pltpu.roll(v, bit, 1))
        return v

    group_mean = over_group(mean) * (1.0 / 8)
    d = mean - group_mean
    variance = over_group(sq + held * d * d) * (1.0 / (8 * held))
    scale = 0.5 * gain[...] / jnp.sqrt(variance + 1e-05)
    shift = (ref_mean[...] - group_mean) * scale + 0.5 * bias[...]
    scale_out[...] = jnp.concatenate([scale] * 4, axis=1)
    shift_out[...] = jnp.concatenate([shift] * 4, axis=1)

    for share in shares:
        share.wait_send()
    for d in range(4):
        last_a(d).wait_send()
        last_b(d).wait_send()
    for s in range(4):
        for copy in out_copies(s):
            copy.wait()
        for d in range(4):
            if s != 2:
                across(s, d).wait_send()
            if s or d:
                plane(s, d).wait_send()
        for c0, n, row in ((0, 6, s),):

            @pl.when(r > 0)
            def _():
                up(s, c0, n, row).wait_send()

            @pl.when(r < 3)
            def _():
                down(s, c0, n, row).wait_send()


def per_device(video, conv_weight, norm_gain, norm_bias):
    vmem = pl.BlockSpec(memory_space=pltpu.VMEM)
    anywhere = pl.BlockSpec(memory_space=pl.ANY)
    dma = pltpu.SemaphoreType.DMA
    conv, scale, shift = pl.pallas_call(
        exchange_conv,
        out_shape=(
            jax.ShapeDtypeStruct((4, 2, 256, 1024), BF16),
            jax.ShapeDtypeStruct((1, 1024), F32),
            jax.ShapeDtypeStruct((1, 1024), F32),
        ),
        in_specs=[anywhere, anywhere, vmem, vmem],
        out_specs=(anywhere, vmem, vmem),
        scratch_shapes=[
            pltpu.VMEM((8, 8, 128, C), BF16),
            pltpu.VMEM((130, 64, C), BF16),
            pltpu.VMEM((4, 4, 10, 64, C), BF16),
            pltpu.VMEM((4, 4, 6, 64, C), BF16),
            pltpu.VMEM((4, 2, 6, 64, C), BF16),
            pltpu.VMEM((4, 2, 6, 64, C), BF16),
            pltpu.VMEM((6, 10, 8 + T_ROWS, C), F32),
            pltpu.VMEM((3, 6, 10, T_ROWS, C), BF16),
            pltpu.VMEM((4, 2, T_ROWS, 1024), BF16),
            pltpu.VMEM((27 * C, CO), BF16),
            pltpu.VMEM((3, 8, CO), F32),
            pltpu.VMEM((24, 1, 2 * CO), F32),
            pltpu.VMEM((1, CO), F32),
            dma((4, 4)), dma((4, 4)),
            dma((5, 4)), dma((5, 4)),
            dma,
            dma((5, 2)), dma((5, 2)),
            dma((2, 16)), dma((2, 16)),
            dma, dma, dma((4, 2)),
        ],
        compiler_params=pltpu.CompilerParams(
            collective_id=0, has_side_effects=True, vmem_limit_bytes=60 << 20
        ),
        cost_estimate=pl.CostEstimate(
            flops=2 * 8192 * 3456 * 256, bytes_accessed=16 << 20, transcendentals=0
        ),
    )(video, conv_weight.reshape(27 * C, CO), norm_gain.reshape(1, CO), norm_bias.reshape(1, CO))
    half = conv.astype(F32) * scale[0] + shift[0]
    return (half + half * jnp.tanh(half)).astype(BF16)


def solution(mesh):
    placed = (P("tm", "rows", None, None), P(), P(), P())
    return jax.shard_map(
        per_device,
        mesh=mesh,
        in_specs=placed,
        out_specs=P("rows", "tm", None, None),
        check_vma=False,
    )
```

time: 92.4 us -> 77.5 us (0.84); the launches traced: 91.1 us -> 77.2 us
  Pallas kernels: 87 us -> 72.4 us
  other arithmetic: 0 us -> 4.71 us
  local copies, waits for them, and re-layouts: 4.13 us -> 0 us
    pallas_call x1, Pallas kernels: 82.6 us -> 72.4 us  [per_device(): pl.pallas_call(exchange_conv, out_shape=(jax.ShapeDtypeStruct((4, 2, 256,...]
    convert_element_type x0 -> x1, other arithmetic: none -> 4.71 us  [per_device(): return (half + half * jnp.tanh(half)).astype(BF16)]
    pallas_call x1 -> x0, Pallas kernels: 4.36 us -> none  [per_device(): pl.pallas_call(norm_silu, out_shape=jax.ShapeDtypeStruct((4, 2, 256, 1024...]
    unnamed x4 -> x0, local copies, waits for them, and re-layouts: 4.13 us -> none
where the time goes in v2:
time: 77.5 us; the launch traced here: 77.2 us
  Pallas kernels  72.4 us (93%)
  other arithmetic  4.71 us (6%)
    pallas_call x1, Pallas kernels, per_device(): pl.pallas_call(exchange_conv, out_shape=(jax.ShapeDtypeStruct((4, 2, 256,...  72.4 us
    convert_element_type x1, other arithmetic, per_device(): return (half + half * jnp.tanh(half)).astype(BF16)  4.71 us

profile of v2, /device:TPU:0, one launch (start us, length us, event | category | flops | bytes accessed | tf_op | source)
XLA Modules:
  0.0 77.2 jit_solution(2736106654407370381)
XLA Ops:
  0.0 72.4 %shard_map.46 = (bf16[4,2,256,1024]{3,2,1,0:T(8,128)(2,1)}, f32[1,1024]{1,0:T(1,128)}, f32[1,1024]{1,0:T(1,128)}) custom-call(bf16[8,8,128,128]{3,2,1,0:T(8,128)(2,1)} %video_in.1, bf16[3456,256]{1,0:T(8,128)(2,1)} %bitcast.7, f32[1,256]{1,0:T(1,128)} %bitcast.8, f32[1,256]{1,0:T(1,128)} %bitcast.9), custom_call_target="tpu_custom_call" | custom-call | flops 14495514624 | bytes 16777216 | tf_op jit(solution)/shard_map/pallas_call | solution.py:409
  72.4 4.7 %fusion = bf16[4,2,256,1024]{3,2,1,0:T(8,128)(2,1)} fusion(bf16[4,2,256,1024]{3,2,1,0:T(8,128)(2,1)} %get-tuple-element.8, f32[1024]{0:T(1024)} %bitcast.6, f32[1024]{0:T(1024)} %bitcast.5), kind=kLoop, calls=%fused_computation.1 | loop fusion | flops 12582912 | bytes 8396800 | tf_op jit(solution)/shard_map/convert_element_type | solution.py:447

commit v3 on v2

--- a/solution.py
+++ b/solution.py
@@ -86,15 +86,9 @@
             send_sem=y_s.at[row, d], recv_sem=y_r.at[row, d],
             device_id=at(z, x, 1 - y), device_id_type=MESH)
 
-    def last_a(d):
-        return across(2, d, False, 0, 4, 2)
-
-    def last_b(d):
-        return across(2, d, False, 4, 2, 4)
-
     def forward(s, d):
         plane(s, d).wait_recv()
-        (last_a(d) if s == 2 else across(s, d)).start()
+        across(s, d).start()
 
     def up(s, c0, n, row):
         return pltpu.make_async_remote_copy(
@@ -302,19 +296,6 @@
         conv_all(s, 0, 4, EDGES, 3)
         finish(s)
 
-    def last_whole(s):
-        for d in range(4):
-            last_a(d).wait_recv()
-            last_b(d).wait_recv()
-        waves(s, 0, 6, s)
-        build_taps(s, 0, 6, 1, 9)
-        conv_pairs(s, None)
-        take_halo(s, 0, 6, s)
-        build_taps(s, 0, 6, 0, 1)
-        build_taps(s, 0, 6, 9, 10)
-        conv_all(s, 0, 4, EDGES, 3)
-        finish(s)
-
     for s, d in ORDER:
         plane(s, d).start()
     own.start()
@@ -329,10 +310,8 @@
     stage(1, hook((3, 2), (2, 0), (2, 1)))
     for d in (3, 2):
         forward(2, d)
-    for d in range(4):
-        last_b(d).start()
     stage(3, None)
-    last_whole(2)
+    stage(2, None)
 
     mean, sq = st[0, 0:1, :], st[0, 1:2, :]
     held = float(done[0])
@@ -380,15 +359,11 @@
 
     for share in shares:
         share.wait_send()
-    for d in range(4):
-        last_a(d).wait_send()
-        last_b(d).wait_send()
     for s in range(4):
         for copy in out_copies(s):
             copy.wait()
         for d in range(4):
-            if s != 2:
-                across(s, d).wait_send()
+            across(s, d).wait_send()
             if s or d:
                 plane(s, d).wait_send()
         for c0, n, row in ((0, 6, s),):

time: 77.5 us -> 76.3 us (0.985)
  Pallas kernels: 72.4 us -> 71.3 us
    pallas_call x1, Pallas kernels: 72.4 us -> 71.3 us  [per_device(): pl.pallas_call(exchange_conv, out_shape=(jax.ShapeDtypeStruct((4, 2, 256,...]
where the time goes in v3:
time: 76.3 us; the launch traced here: 76.1 us
  Pallas kernels  71.3 us (93%)
  other arithmetic  4.71 us (6%)
    pallas_call x1, Pallas kernels, per_device(): pl.pallas_call(exchange_conv, out_shape=(jax.ShapeDtypeStruct((4, 2, 256,...  71.3 us
    convert_element_type x1, other arithmetic, per_device(): return (half + half * jnp.tanh(half)).astype(BF16)  4.71 us

profile of v3, /device:TPU:0, one launch (start us, length us, event | category | flops | bytes accessed | tf_op | source)
XLA Modules:
  0.0 76.1 jit_solution(5013183941778257679)
XLA Ops:
  0.0 71.3 %shard_map.46 = (bf16[4,2,256,1024]{3,2,1,0:T(8,128)(2,1)}, f32[1,1024]{1,0:T(1,128)}, f32[1,1024]{1,0:T(1,128)}) custom-call(bf16[8,8,128,128]{3,2,1,0:T(8,128)(2,1)} %video_in.1, bf16[3456,256]{1,0:T(8,128)(2,1)} %bitcast.7, f32[1,256]{1,0:T(1,128)} %bitcast.8, f32[1,256]{1,0:T(1,128)} %bitcast.9), custom_call_target="tpu_custom_call" | custom-call | flops 14495514624 | bytes 16777216 | tf_op jit(solution)/shard_map/pallas_call | solution.py:384
  71.4 4.7 %fusion = bf16[4,2,256,1024]{3,2,1,0:T(8,128)(2,1)} fusion(bf16[4,2,256,1024]{3,2,1,0:T(8,128)(2,1)} %get-tuple-element.8, f32[1024]{0:T(1024)} %bitcast.6, f32[1024]{0:T(1024)} %bitcast.5), kind=kLoop, calls=%fused_computation.1 | loop fusion | flops 12582912 | bytes 8396800 | tf_op jit(solution)/shard_map/convert_element_type | solution.py:422
